TPU v7x, 256 devices: a whole 4x4x8 slice. The times are simulated.
256 devices in a mesh: tm: 16 (over x, z_hi, core), win: 4 (over z_lo), space: 4 (over y).
Axes of the slice: x: 4, y: 4, z: 8 (z_hi: 2, z_lo: 4; z = z_hi * 4 + z_lo), core: 2. Of those that a mesh axis runs over, the one named last changes fastest.
Arguments:
- states: float32 [4, 16, 3, 256, 2048], P('win', 'tm', None, 'space'), may hold values from -4 to 4
- initial_state: float32 [3, 256, 2048], P(None, 'space'), may hold values from -4 to 4
Outputs:
- coeffs: float32 [4, 9, 256, 2048], P('win', None, 'space')
- residual: float32 [4, 16, 3, 256, 2048], P('win', 'tm', None, 'space')
All inputs are finite; a program needn't handle non-finite values.
Results may differ from a plain program's by a relative error of at most 0.00002.
Values sent between devices are 32-bit elements; how exact they have to be, the bound alone decides.
No kernel may reach another device: no remote copies, remote signals or barrier semaphores. Data moves between devices by JAX's collectives and lax.ppermute only.
A program may use at most 64 MiB of HBM per device.

v0:
```python
import jax
import jax.numpy as jnp
from jax import lax
from jax.sharding import PartitionSpec as P

mean_depth = 1.0
coriolis_rate = 1.0
grav_accel = 1.0
time_step = 0.5


def extended(cells, sides, width):
    for axis, dim in sides:
        count = lax.axis_size(axis)
        head = lax.slice_in_dim(cells, 0, width, axis=dim)
        tail = lax.slice_in_dim(cells, cells.shape[dim] - width, cells.shape[dim], axis=dim)
        cells = jnp.concatenate(
            [
                lax.ppermute(tail, axis, [(i, (i + 1) % count) for i in range(count)]),
                cells,
                lax.ppermute(head, axis, [((i + 1) % count, i) for i in range(count)]),
            ],
            axis=dim,
        )
    return cells


def shifted(value, axis, by):
    peers = lax.axis_size(axis)
    return lax.ppermute(value, axis, [(i, (i + by) % peers) for i in range(peers)])


def shifted_2(value, axis, steps):
    count = lax.axis_size(axis)
    leading, last = (max(0, -steps), min(count, count - steps))
    return lax.ppermute(value, axis, [(source, source + steps) for source in range(leading, last)])


def local_coeffs(padded):
    inner = padded[:, 1:-1]
    ddx = (jnp.roll(inner, -1, -1) - jnp.roll(inner, 1, -1)) * 0.5
    ddy = (padded[:, 2:] - padded[:, :-2]) * 0.5
    return jnp.stack(
        [inner[0], inner[1], mean_depth + inner[2], ddx[0], ddy[0], ddx[1], ddy[1], ddx[2], ddy[2]],
        axis=0,
    )


def tendency(fields):
    speed_u, speed_v, depth = (fields[0], fields[1], fields[2])
    u_dx, u_dy, v_dx, v_dy = (fields[3], fields[4], fields[5], fields[6])
    e_dx, e_dy = (fields[7], fields[8])
    force_u = -speed_u * u_dx - speed_v * u_dy + coriolis_rate * speed_v - grav_accel * e_dx
    force_v = -speed_u * v_dx - speed_v * v_dy - coriolis_rate * speed_u - grav_accel * e_dy
    force_e = -(depth * u_dx + speed_u * e_dx) - (depth * v_dy + speed_v * e_dy)
    return jnp.stack([force_u, force_v, force_e], axis=0)


def shards(states, initial_state):
    current = states[0, 0]
    padded = extended(current, (("space", 1),), 1)
    fields = local_coeffs(padded)
    step_count = lax.axis_size("tm")
    totals = lax.psum(fields, "tm")
    averaged = totals / step_count
    before = shifted(current, "tm", 1)
    carried = shifted_2(before, "win", 1)
    first_step = lax.axis_index("tm") == 0
    first_window = lax.axis_index("win") == 0
    handed = jnp.where(first_window, initial_state, carried)
    earlier = jnp.where(first_step, handed, before)
    left = current - earlier - time_step * tendency(fields)
    return (averaged[None], left[None, None])


def solution(mesh):
    in_specs = (P("win", "tm", None, "space", None), P(None, "space", None))
    out_specs = (P("win", None, "space", None), P("win", "tm", None, "space", None))
    return jax.shard_map(shards, mesh=mesh, in_specs=in_specs, out_specs=out_specs, check_vma=False)
```

profile of v0, /device:TPU:26, one launch (start us, length us, event | category | flops | bytes accessed | tf_op | source)
XLA Modules:
  0.0 321.4 jit_solution(13687084732740321212)
XLA Ops:
  7.2 0.0 all-reduce.2.cloned.1.call-start
  7.2 1.1 fusion.14
  8.3 0.3 collective-permute-start.1
  8.6 1.8 collective-permute-start
  10.4 1.0 fusion.15
  11.4 0.0 copy-start
  11.4 2.6 fusion.16
  14.0 0.0 copy-done
  14.1 0.8 bitcast_dynamic-update-slice_fusion.2
  14.9 0.5 fusion.2
  15.4 0.0 collective-permute-done.1
  15.4 0.0 collective-permute-done
  15.5 0.4 fusion.1
  15.8 1.2 fusion.10
  17.0 0.8 bitcast_dynamic-update-slice_fusion
  17.8 0.8 slice_dynamic-update-slice_fusion.5
  18.7 0.8 slice_dynamic-update-slice_fusion.1
  19.5 0.8 slice_dynamic-update-slice_fusion
  20.3 0.8 slice_dynamic-update-slice_fusion.4
  21.2 0.8 slice_dynamic-update-slice_fusion.3
  22.0 0.8 slice_dynamic-update-slice_fusion.2
  22.8 0.0 all-reduce.2.cloned.1.call-update
  22.8 0.1 collective-permute-start.2
  22.9 45.1 %collective-permute-done.2 = f32[3,64,2048]{2,1,0:T(8,128)} collective-permute-done((f32[3,64,2048]{2,1,0:T(8,128)S(1)}, f32[3,64,2048]{2,1,0:T(8,128)}, u32[]{:S(2)}, u32[]{:S(2)}) %collective-permute-start.2) | collective-permute-done | bytes 1572896 | tf_op jit(solution)/shard_map/ppermute | solution.py:30
  68.0 27.0 %collective-permute-start.3 = (f32[3,64,2048]{2,1,0:T(8,128)}, f32[3,64,2048]{2,1,0:T(8,128)}, u32[]{:S(2)}, u32[]{:S(2)}) collective-permute-start(f32[3,64,2048]{2,1,0:T(8,128)} %collective-permute-done.2), channel_id=1, source_target_pairs={{0,4},{4,8},{8,12},{1,5},{5,9},{9,13},{2,6},{6,10},{10,14},{3,7},{... | collective-permute-start | bytes 4718600 | tf_op jit(solution)/shard_map/ppermute | solution.py:36
  95.0 98.0 %collective-permute-done.3 = f32[3,64,2048]{2,1,0:T(8,128)} collective-permute-done((f32[3,64,2048]{2,1,0:T(8,128)}, f32[3,64,2048]{2,1,0:T(8,128)}, u32[]{:S(2)}, u32[]{:S(2)}) %collective-permute-start.3) | collective-permute-done | bytes 1572896 | tf_op jit(solution)/shard_map/ppermute | solution.py:36
  193.0 3.9 %fusion.4 = f32[1,1,3,64,2048]{4,3,2,1,0:T(8,128)} fusion(f32[1,64,2048]{2,1,0:T(8,128)S(1)} %get-tuple-element.4, f32[1,64,2048]{2,1,0:T(8,128)S(1)} %get-tuple-element.3, f32[1,64,2048]{2,1,0:T(8,128)S(1)} %get-tuple-element.2, f32[3,64,2048]{2,1,0:T(8,128)} %collective-permute-done.2, f32[3,64,2048]{2,1,0:T(8,128)} %param.3, ...), kind=kLoop, calls=%fused_computation.9 | loop fusion | flops 2752512 | bytes 9437186 | tf_op jit(solution)/shard_map/broadcast_in_dim | solution.py:73
  196.9 112.3 %all-reduce.2.cloned.1.call-done = f32[9,64,2048]{2,1,0:T(8,128)} async-done(((f32[9,64,2048]{2,1,0:T(8,128)}), f32[9,64,2048]{2,1,0:T(8,128)}) %all-reduce.2.cloned.1.call-update) | async-done | bytes 4718608 | tf_op jit(solution)/shard_map/psum | solution.py:64
  309.3 5.2 %multiply_bitcast_fusion = f32[1,9,64,2048]{3,2,1,0:T(8,128)} fusion(f32[9,64,2048]{2,1,0:T(8,128)} %all-reduce.2.cloned.1.call-done), kind=kLoop, calls=%fused_computation | loop fusion | flops 1179648 | bytes 9437184 | tf_op jit(solution)/shard_map/broadcast_in_dim | solution.py:73
Async XLA Ops:
  7.2 302.1 %all-reduce.2.cloned.1.call-start = ((), (), s32[]{:S(2)}) async-start(), calls=%async_computation | async-start | bytes 9437184 | tf_op jit(solution)/shard_map/psum | solution.py:64
  8.3 7.2 %collective-permute-start.1 = (f32[3,1,2048]{2,1,0:T(1,128)S(1)}, f32[3,1,2048]{2,1,0:T(1,128)S(1)}, u32[]{:S(2)}, u32[]{:S(2)}) collective-permute-start(f32[3,1,2048]{2,1,0:T(1,128)S(1)} %get-tuple-element.7), channel_id=1, source_target_pairs={{0,1},{1,2},{2,3},{3,0},{4,5},{5,6},{6,7},{7,4},{8,9},{9,10},{10,1... | collective-permute-start | bytes 73736 | tf_op jit(solution)/shard_map/ppermute | solution.py:19
  8.6 6.9 %collective-permute-start = (f32[3,1,2048]{2,1,0:T(1,128)S(1)}, f32[3,1,2048]{2,1,0:T(1,128)S(1)}, u32[]{:S(2)}, u32[]{:S(2)}) collective-permute-start(f32[3,1,2048]{2,1,0:T(1,128)S(1)} %get-tuple-element.6), channel_id=1, source_target_pairs={{1,0},{2,1},{3,2},{0,3},{5,4},{6,5},{7,6},{4,7},{9,8},{10,9},{11,1... | collective-permute-start | bytes 73736 | tf_op jit(solution)/shard_map/ppermute | solution.py:21
  11.4 2.6 copy-start
  22.8 45.2 %collective-permute-start.2 = (f32[3,64,2048]{2,1,0:T(8,128)S(1)}, f32[3,64,2048]{2,1,0:T(8,128)}, u32[]{:S(2)}, u32[]{:S(2)}) collective-permute-start(f32[3,64,2048]{2,1,0:T(8,128)S(1)} %bitcast.55), channel_id=1, source_target_pairs={{0,16},{16,32},{32,48},{48,64},{64,80},{80,96},{96,112},{112,128},... | collective-permute-start | bytes 4718600 | tf_op jit(solution)/shard_map/ppermute | solution.py:30
  68.0 125.0 %collective-permute-start.3 = (f32[3,64,2048]{2,1,0:T(8,128)}, f32[3,64,2048]{2,1,0:T(8,128)}, u32[]{:S(2)}, u32[]{:S(2)}) collective-permute-start(f32[3,64,2048]{2,1,0:T(8,128)} %collective-permute-done.2), channel_id=1, source_target_pairs={{0,4},{4,8},{8,12},{1,5},{5,9},{9,13},{2,6},{6,10},{10,14},{3,7},{... | collective-permute-start | bytes 4718600 | tf_op jit(solution)/shard_map/ppermute | solution.py:36
Sparse Core Ops, SparseCore 0:
  23.0 286.2 all-reduce.1
where the time goes:
time: 327 us; the launch traced here: 321 us
  waiting for transfers between devices  255 us (78%)
  starting transfers between devices  29.2 us (9%)
  between operations  14.1 us (4%)
  other arithmetic  12.1 us (4%)
  local copies, waits for them, and re-layouts  10.5 us (3%)
    psum x1, waiting for transfers between devices, shards(): totals = lax.psum(fields, 'tm')  112 us
    ppermute x1, waiting for transfers between devices, shifted_2(): lax.ppermute(value, axis, [(source, source + steps) for source in range(l...  98 us
    ppermute x1, waiting for transfers between devices, shifted(): lax.ppermute(value, axis, [(i, (i + by) % peers) for i in range(peers)])  45.1 us
    ppermute x1, starting transfers between devices, shifted_2(): lax.ppermute(value, axis, [(source, source + steps) for source in range(l...  27 us
    broadcast_in_dim x2, other arithmetic, shards(): return (averaged[None], left[None, None])  9.16 us
  transfers between devices with their start and end apart: 5, of which 3 were waited for; matrix products, arithmetic and copies ran while one was open for 3% of the time, Pallas kernels for 0%

commit v1 on v0

v1 whole, which is shorter than its diff:
```python
import jax
import jax.numpy as jnp
from jax import lax
from jax.experimental import pallas as pl
from jax.experimental.pallas import tpu as pltpu
from jax.sharding import PartitionSpec as P

AXES = ("tm", "win", "space")
VMEM_BYTES = 24 * 1024 * 1024


def place(x, z, y, core):
    z_hi, z_lo = divmod(z % 8, 4)
    tm = ((x % 4) * 2 + z_hi) * 2 + core
    return (tm * 4 + z_lo) * 4 + y % 4


def pairs(target):
    found = []
    for x in range(4):
        for z in range(8):
            for y in range(4):
                for core in range(2):
                    to = target(x, z, y, core)
                    if to is not None:
                        found.append((place(x, z, y, core), place(*to)))
    return found


def send(value, target):
    return lax.ppermute(value, AXES, pairs(target))


def step_target(x, z, y, core):
    if core == 0:
        return None
    if z < 4:
        return (x, z + 4, y, 0)
    if x < 3:
        return (x + 1, z - 4, y, 0)
    return {4: (0, 1, y, 0), 5: (3, 7, y, 1), 6: (0, 3, y, 0), 7: None}[z]


def relay_target(x, z, y, core):
    return (0, 2, y, 0) if (x, z, core) == (3, 7, 1) else None


def swap_target(x, z, y, core):
    return (x, z, y, 1 - core)


def x_target(by):
    return lambda x, z, y, core: (x + by, z, y, core)


def z_target(x, z, y, core):
    return (x, z + 4, y, core)


def up_target(x, z, y, core):
    return (x, z, y + 1, core)


def down_target(x, z, y, core):
    return (x, z, y - 1, core)


def edge_target(flip):
    def target(x, z, y, core):
        return (x, z, y - 1 if core == 0 else y + 1, core ^ flip)

    return target


def params():
    return pltpu.CompilerParams(vmem_limit_bytes=VMEM_BYTES)


def ddx(value):
    width = value.shape[1]
    return (pltpu.roll(value, width - 1, 1) - pltpu.roll(value, 1, 1)) * 0.5


def ddy(above, value, below):
    row = lax.broadcasted_iota(jnp.int32, value.shape, 0)
    after = jnp.where(row == 7, pltpu.roll(below, 7, 0), pltpu.roll(value, 7, 0))
    before = jnp.where(row == 0, pltpu.roll(above, 1, 0), pltpu.roll(value, 1, 0))
    return (after - before) * 0.5


def split_kernel(where_ref, *refs):
    for k in range(4):
        refs[8 + k][...] = (refs[k][...] + refs[4 + k][...])[:, 0]


def split_sum(where, own, other):
    own, other = (a.reshape(3, 8, 8, -1) for a in (own, other))
    cols = own.shape[-1]

    def spec(k):
        return pl.BlockSpec((3, 1, 8, cols), lambda i, w: (0, w[1] * 4 + (w[0] + k) % 4, 0, 0))

    piece = pl.BlockSpec((3, 8, cols), lambda i, w: (0, 0, 0))
    return pl.pallas_call(
        split_kernel,
        grid_spec=pltpu.PrefetchScalarGridSpec(
            num_scalar_prefetch=1,
            grid=(1,),
            in_specs=[spec(k) for k in range(4)] * 2,
            out_specs=[piece] * 4,
        ),
        out_shape=[jax.ShapeDtypeStruct((3, 8, cols), jnp.float32)] * 4,
        compiler_params=params(),
        name="split_sum",
    )(where, *([own] * 4), *([other] * 4))


def gather_kernel(where_ref, p0, p1, p2, p3, half_ref, edge_ref):
    x, core = where_ref[0], where_ref[1]
    for k, piece in enumerate((p0, p1, p2, p3)):
        slot = (x + k) % 4
        half_ref[:, slot] = piece[...]

        @pl.when((core == 0) & (slot == 0))
        def _():
            edge_ref[...] = piece[:, 0:1]

        @pl.when((core == 1) & (slot == 3))
        def _():
            edge_ref[...] = piece[:, 7:8]


def gather(where, pieces):
    cols = pieces[0].shape[-1]
    vmem = pl.BlockSpec(memory_space=pltpu.VMEM)
    return pl.pallas_call(
        gather_kernel,
        in_specs=[pl.BlockSpec(memory_space=pltpu.SMEM)] + [vmem] * 4,
        out_specs=[vmem] * 2,
        out_shape=[
            jax.ShapeDtypeStruct((3, 4, 8, cols), jnp.float32),
            jax.ShapeDtypeStruct((3, 1, cols), jnp.float32),
        ],
        compiler_params=params(),
        name="gather",
    )(where, *pieces)


def coeffs_kernel(where_ref, half_ref, other_ref, near_ref, far_ref, out_ref, mean):
    step = pl.program_id(0)

    @pl.when(step == 0)
    def _():
        core = where_ref[1]
        mean[:, pl.ds(1 + core * 4, 4)] = half_ref[...]
        mean[:, pl.ds(5 - core * 4, 4)] = other_ref[...]

        @pl.when(core == 0)
        def _():
            mean[:, 9, 0:1] = near_ref[...]
            mean[:, 0, 7:8] = far_ref[...]

        @pl.when(core == 1)
        def _():
            mean[:, 0, 7:8] = near_ref[...]
            mean[:, 9, 0:1] = far_ref[...]

    for f in range(3):
        value = mean[f, step + 1]
        out_ref[f] = value + 1.0 if f == 2 else value
        out_ref[3 + 2 * f] = ddx(value)
        out_ref[4 + 2 * f] = ddy(mean[f, step], value, mean[f, step + 2])


def coeffs_of(where, half, other, near, far):
    cols = half.shape[-1]

    def whole(a):
        return pl.BlockSpec(a.shape, lambda i, w: (0,) * a.ndim)

    return pl.pallas_call(
        coeffs_kernel,
        grid_spec=pltpu.PrefetchScalarGridSpec(
            num_scalar_prefetch=1,
            grid=(8,),
            in_specs=[whole(a) for a in (half, other, near, far)],
            out_specs=pl.BlockSpec((9, 8, cols), lambda i, w: (0, i, 0)),
            scratch_shapes=[pltpu.VMEM((3, 10, 8, cols), jnp.float32)],
        ),
        out_shape=jax.ShapeDtypeStruct((9, 64, cols), jnp.float32),
        compiler_params=params(),
        name="coeffs",
    )(where, half, other, near, far)


def local_kernel(state_ref, above_ref, below_ref, out_ref):
    def block(f, r):
        if r < 0:
            return jnp.broadcast_to(above_ref[f], (8, above_ref.shape[-1]))
        if r > 7:
            return jnp.broadcast_to(below_ref[f], (8, below_ref.shape[-1]))
        return state_ref[f, r]

    for r in range(8):
        u, v, e = (state_ref[f, r] for f in range(3))
        dx = [ddx(w) for w in (u, v, e)]
        dy = [ddy(block(f, r - 1), w, block(f, r + 1)) for f, w in enumerate((u, v, e))]
        force_u = -u * dx[0] - v * dy[0] + v - dx[2]
        force_v = -u * dx[1] - v * dy[1] - u - dy[2]
        depth = 1.0 + e
        force_e = -(depth * dx[0] + u * dx[2]) - (depth * dy[1] + v * dy[2])
        out_ref[0, r] = u - 0.5 * force_u
        out_ref[1, r] = v - 0.5 * force_v
        out_ref[2, r] = e - 0.5 * force_e


def local_part(state, above, below):
    cols = state.shape[-1]
    vmem = pl.BlockSpec(memory_space=pltpu.VMEM)
    return pl.pallas_call(
        local_kernel,
        in_specs=[vmem] * 3,
        out_specs=vmem,
        out_shape=jax.ShapeDtypeStruct((3, 8, 8, cols), jnp.float32),
        compiler_params=params(),
        name="local_part",
    )(state.reshape(3, 8, 8, cols), above, below)


def residual_kernel(which_ref, local_ref, *refs):
    out_ref = refs[-1]
    for k, previous in enumerate(refs[:-1]):

        @pl.when(which_ref[0] == k)
        def _():
            out_ref[...] = local_ref[...] - previous[...]


def residual_of(which, local, candidates):
    cols = local.shape[-1]

    def spec(k):
        return pl.BlockSpec((1, 64, cols), lambda i, w: (jnp.where(w[0] == k, i, 0), 0, 0))

    block = pl.BlockSpec((1, 64, cols), lambda i, w: (i, 0, 0))
    return pl.pallas_call(
        residual_kernel,
        grid_spec=pltpu.PrefetchScalarGridSpec(
            num_scalar_prefetch=1,
            grid=(3,),
            in_specs=[block] + [spec(k) for k in range(len(candidates))],
            out_specs=block,
        ),
        out_shape=jax.ShapeDtypeStruct((3, 64, cols), jnp.float32),
        compiler_params=params(),
        name="residual",
    )(which, local, *candidates)


def shards(states, initial_state):
    current = states[0, 0]
    cols = current.shape[-1]
    step, window = lax.axis_index("tm"), lax.axis_index("win")
    x, core = step // 4, step % 2
    where = jnp.stack([x, core]).astype(jnp.int32)

    other = send(current, swap_target)
    far = send(current, step_target)
    above = send(current[:, 63:64], up_target)
    below = send(current[:, 0:1], down_target)

    pieces = split_sum(where, current, other)
    came = [send(pieces[k], x_target(k)) for k in (1, 3, 2)]
    part = (pieces[0] + came[0]) + (came[1] + came[2])
    part = (part + send(part, z_target)) * (1.0 / 16.0)
    gathered = [part] + [send(part, x_target(-k)) for k in (1, 2, 3)]
    half, edge = gather(where, gathered)
    other_half = send(half, swap_target)
    near = send(edge, edge_target(0))
    beyond = send(edge, edge_target(1))
    coeffs = coeffs_of(where, half, other_half, near, beyond)

    local = local_part(current, above, below).reshape(3, 64, cols)
    relayed = send(far, relay_target)
    first = jnp.where(window == 0, 3, jnp.where(window == 2, 2, 1))
    which = jnp.where(core == 1, 0, jnp.where(step == 0, first, 1)).astype(jnp.int32).reshape(1)
    residual = residual_of(which, local, (other, far, relayed, initial_state))
    return coeffs[None], residual[None, None]


def solution(mesh):
    in_specs = (P("win", "tm", None, "space", None), P(None, "space", None))
    out_specs = (P("win", None, "space", None), P("win", "tm", None, "space", None))
    return jax.shard_map(shards, mesh=mesh, in_specs=in_specs, out_specs=out_specs, check_vma=False)
```

time: 327 us -> 91.8 us (0.28); the launches traced: 321 us -> 91.6 us
  waiting for transfers between devices: 255 us -> 40 us
  between operations: 14.1 us -> 0.73 us
  Pallas kernels: 0 us -> 13.1 us
  other arithmetic: 12.1 us -> 0.14 us
  local copies, waits for them, and re-layouts: 10.5 us -> 1.46 us
  starting transfers between devices: 29.2 us -> 36.2 us
    psum x1 -> x0, waiting for transfers between devices: 112 us -> none  [shards(): totals = lax.psum(fields, 'tm')]
    ppermute x4 -> x15, waiting for transfers between devices: 143 us -> 40 us  [send(): return lax.ppermute(value, AXES, pairs(target))]
    pallas_call x0 -> x5, Pallas kernels: none -> 13.1 us  [the longest x1 6.19 us: coeffs_of(): pl.pallas_call(coeffs_kernel, grid_spec=pltpu.PrefetchScalarGridSpec(num_...]
    broadcast_in_dim x2 -> x0, other arithmetic: 9.16 us -> none  [shards(): return (averaged[None], left[None, None])]
    ppermute x4 -> x15, starting transfers between devices: 29.2 us -> 36.2 us  [send(): return lax.ppermute(value, AXES, pairs(target))]
    slice x3 -> x1, local copies, waits for them, and re-layouts: 4.71 us -> 0.04 us  [shards(): below = send(current[:, 0:1], down_target)]
    unnamed x8 -> x6, local copies, waits for them, and re-layouts: 4.98 us -> 1.42 us
  transfers between devices with their start and end apart: 5 -> 15, of which waited for: 3 -> 10; matrix products, arithmetic and copies ran while one was open for 3% -> 0% of each run, Pallas kernels for 0% -> 10%
where the time goes in v1:
time: 91.8 us; the launch traced here: 91.6 us
  waiting for transfers between devices  40 us (44%)
  starting transfers between devices  36.2 us (39%)
  Pallas kernels  13.1 us (14%)
  local copies, waits for them, and re-layouts  1.46 us (2%)
    ppermute x15, waiting for transfers between devices, send(): return lax.ppermute(value, AXES, pairs(target))  40 us
    ppermute x15, starting transfers between devices, send(): return lax.ppermute(value, AXES, pairs(target))  36.2 us
    pallas_call x1, Pallas kernels, coeffs_of(): pl.pallas_call(coeffs_kernel, grid_spec=pltpu.PrefetchScalarGridSpec(num_...  6.19 us
    pallas_call x1, Pallas kernels, residual_of(): pl.pallas_call(residual_kernel, grid_spec=pltpu.PrefetchScalarGridSpec(nu...  3.6 us
  transfers between devices with their start and end apart: 15, of which 10 were waited for; matrix products, arithmetic and copies ran while one was open for 0% of the time, Pallas kernels for 10%

profile of v1, /device:TPU:26, one launch (start us, length us, event | category | flops | bytes accessed | tf_op | source)
XLA Modules:
  0.0 91.6 jit_solution(3973838234955931717)
XLA Ops:
  0.6 0.1 collective-permute-start
  0.7 1.3 %collective-permute-start.13 = (f32[3,64,2048]{2,1,0:T(8,128)}, f32[3,64,2048]{2,1,0:T(8,128)}, u32[]{:S(2)}, u32[]{:S(2)}) collective-permute-start(f32[3,64,2048]{2,1,0:T(8,128)} %bitcast.10), channel_id=1, source_target_pairs={{16,32},{17,33},{18,34},{19,35},{20,36},{21,37},{22,38},{23,39},{2... | collective-permute-start | bytes 4718600 | tf_op jit(solution)/shard_map/ppermute | solution.py:31
  2.1 0.1 pad_add_fusion.where_ref
  2.1 2.2 %collective-permute-done.refs_0_ = f32[3,64,2048]{2,1,0:T(8,128)S(1)} collective-permute-done((f32[3,64,2048]{2,1,0:T(8,128)}, f32[3,64,2048]{2,1,0:T(8,128)S(1)}, u32[]{:S(2)}, u32[]{:S(2)}) %collective-permute-start) | collective-permute-done | bytes 1572896 | tf_op jit(solution)/shard_map/ppermute | solution.py:31
  4.3 0.0 copy-start
  4.3 1.4 %copy-done = f32[1,1,3,64,2048]{4,3,2,1,0:T(8,128)S(1)} copy-done((f32[1,1,3,64,2048]{4,3,2,1,0:T(8,128)S(1)}, f32[1,1,3,64,2048]{4,3,2,1,0:T(8,128)}, u32[]{:S(2)}) %copy-start) | copy-done | bytes 1572888
  5.7 0.6 split_sum.1
  6.4 0.0 copy-start.1
  6.4 1.6 %collective-permute-start.1 = (f32[3,8,2048]{2,1,0:T(8,128)S(1)}, f32[3,8,2048]{2,1,0:T(8,128)S(1)}, u32[]{:S(2)}, u32[]{:S(2)}) collective-permute-start(f32[3,8,2048]{2,1,0:T(8,128)S(1)} %get-tuple-element.9), channel_id=1, source_target_pairs={{0,64},{16,80},{1,65},{17,81},{2,66},{18,82},{3,67},{19,83},{4,68}... | collective-permute-start | bytes 589832 | tf_op jit(solution)/shard_map/ppermute | solution.py:31
  8.0 0.5 collective-permute-start.2
  8.5 2.1 %collective-permute-start.3 = (f32[3,8,2048]{2,1,0:T(8,128)S(1)}, f32[3,8,2048]{2,1,0:T(8,128)S(1)}, u32[]{:S(2)}, u32[]{:S(2)}) collective-permute-start(f32[3,8,2048]{2,1,0:T(8,128)S(1)} %get-tuple-element.11), channel_id=1, source_target_pairs={{0,128},{16,144},{1,129},{17,145},{2,130},{18,146},{3,131},{19,147... | collective-permute-start | bytes 589832 | tf_op jit(solution)/shard_map/ppermute | solution.py:31
  10.6 15.4 %collective-permute-done.1 = f32[3,8,2048]{2,1,0:T(8,128)S(1)} collective-permute-done((f32[3,8,2048]{2,1,0:T(8,128)S(1)}, f32[3,8,2048]{2,1,0:T(8,128)S(1)}, u32[]{:S(2)}, u32[]{:S(2)}) %collective-permute-start.1) | collective-permute-done | bytes 196640 | tf_op jit(solution)/shard_map/ppermute | solution.py:31
  26.0 0.0 collective-permute-done.2
  26.0 0.0 collective-permute-done.3
  26.1 0.7 collective-permute-start.4
  26.8 5.5 %collective-permute-done.13.refs_1_ = f32[3,64,2048]{2,1,0:T(8,128)} collective-permute-done((f32[3,64,2048]{2,1,0:T(8,128)}, f32[3,64,2048]{2,1,0:T(8,128)}, u32[]{:S(2)}, u32[]{:S(2)}) %collective-permute-start.13) | collective-permute-done | bytes 1572896 | tf_op jit(solution)/shard_map/ppermute | solution.py:31
  32.3 1.8 %collective-permute-start.14 = (f32[3,64,2048]{2,1,0:T(8,128)}, f32[3,64,2048]{2,1,0:T(8,128)}, u32[]{:S(2)}, u32[]{:S(2)}) collective-permute-start(f32[3,64,2048]{2,1,0:T(8,128)} %collective-permute-done.13.refs_1_), channel_id=1, source_target_pairs={{252,8},{253,9},{254,10},{255,11}} | collective-permute-start | bytes 4718600 | tf_op jit(solution)/shard_map/ppermute | solution.py:31
  34.1 1.7 %collective-permute-done.4 = f32[3,8,2048]{2,1,0:T(8,128)S(1)} collective-permute-done((f32[3,8,2048]{2,1,0:T(8,128)S(1)}, f32[3,8,2048]{2,1,0:T(8,128)S(1)}, u32[]{:S(2)}, u32[]{:S(2)}) %collective-permute-start.4) | collective-permute-done | bytes 196640 | tf_op jit(solution)/shard_map/ppermute | solution.py:31
  35.9 22.5 %collective-permute-start.7 = (f32[3,8,2048]{2,1,0:T(8,128)S(1)}, f32[3,8,2048]{2,1,0:T(8,128)S(1)}, u32[]{:S(2)}, u32[]{:S(2)}) collective-permute-start(f32[3,8,2048]{2,1,0:T(8,128)S(1)} %add_multiply_fusion.p0), channel_id=1, source_target_pairs={{0,64},{16,80},{1,65},{17,81},{2,66},{18,82},{3,67},{19,83},{4,68}... | collective-permute-start | bytes 589832 | tf_op jit(solution)/shard_map/ppermute | solution.py:31
  58.4 1.1 %collective-permute-start.6 = (f32[3,8,2048]{2,1,0:T(8,128)S(1)}, f32[3,8,2048]{2,1,0:T(8,128)S(1)}, u32[]{:S(2)}, u32[]{:S(2)}) collective-permute-start(f32[3,8,2048]{2,1,0:T(8,128)S(1)} %add_multiply_fusion.p0), channel_id=1, source_target_pairs={{0,128},{16,144},{1,129},{17,145},{2,130},{18,146},{3,131},{19,147... | collective-permute-start | bytes 589832 | tf_op jit(solution)/shard_map/ppermute | solution.py:31
  59.5 1.1 %collective-permute-start.5 = (f32[3,8,2048]{2,1,0:T(8,128)S(1)}, f32[3,8,2048]{2,1,0:T(8,128)S(1)}, u32[]{:S(2)}, u32[]{:S(2)}) collective-permute-start(f32[3,8,2048]{2,1,0:T(8,128)S(1)} %add_multiply_fusion.p0), channel_id=1, source_target_pairs={{0,192},{16,208},{1,193},{17,209},{2,194},{18,210},{3,195},{19,211... | collective-permute-start | bytes 589832 | tf_op jit(solution)/shard_map/ppermute | solution.py:31
  60.6 6.5 %collective-permute-done.7.p3 = f32[3,8,2048]{2,1,0:T(8,128)S(1)} collective-permute-done((f32[3,8,2048]{2,1,0:T(8,128)S(1)}, f32[3,8,2048]{2,1,0:T(8,128)S(1)}, u32[]{:S(2)}, u32[]{:S(2)}) %collective-permute-start.7) | collective-permute-done | bytes 196640 | tf_op jit(solution)/shard_map/ppermute | solution.py:31
  67.1 0.6 collective-permute-done.6.p2
  67.7 2.4 %collective-permute-done.5.p1 = f32[3,8,2048]{2,1,0:T(8,128)S(1)} collective-permute-done((f32[3,8,2048]{2,1,0:T(8,128)S(1)}, f32[3,8,2048]{2,1,0:T(8,128)S(1)}, u32[]{:S(2)}, u32[]{:S(2)}) %collective-permute-start.5) | collective-permute-done | bytes 196640 | tf_op jit(solution)/shard_map/ppermute | solution.py:31
  70.1 1.5 %gather.1 = (f32[3,4,8,2048]{3,2,1,0:T(8,128)}, f32[3,1,2048]{2,1,0:T(1,128)S(1)}) custom-call(s32[2]{0:T(128)S(1)} %pad_add_fusion.where_ref, f32[3,8,2048]{2,1,0:T(8,128)S(1)} %add_multiply_fusion.p0, f32[3,8,2048]{2,1,0:T(8,128)S(1)} %collective-permute-done.5.p1, f32[3,8,2048]{2,1,0:T(8,128)S(1)} %collective-permute-done.6.p2, ...), custom_call_target="tpu_custom_call" | custom-call | tf_op jit(solution)/shard_map/gather/pallas_call | solution.py:136
  71.6 0.0 collective-permute-start.8
  71.6 0.0 copy-done.1
  71.7 0.8 collective-permute-start.12
  72.5 2.5 %collective-permute-start.11 = (f32[3,1,2048]{2,1,0:T(1,128)S(1)}, f32[3,1,2048]{2,1,0:T(1,128)S(1)}, u32[]{:S(2)}, u32[]{:S(2)}) collective-permute-start(f32[3,1,2048]{2,1,0:T(1,128)S(1)} %get-tuple-element.15), channel_id=1, source_target_pairs={{0,1},{16,17},{1,2},{17,18},{2,3},{18,19},{3,0},{19,16},{4,5},{20,... | collective-permute-start | bytes 73736 | tf_op jit(solution)/shard_map/ppermute | solution.py:31
  75.0 0.0 collective-permute-start.10
  75.0 1.8 %collective-permute-done.12.below_ref = f32[3,1,2048]{2,1,0:T(1,128)S(1)} collective-permute-done((f32[3,1,2048]{2,1,0:T(1,128)S(1)}, f32[3,1,2048]{2,1,0:T(1,128)S(1)}, u32[]{:S(2)}, u32[]{:S(2)}) %collective-permute-start.12) | collective-permute-done | bytes 24608 | tf_op jit(solution)/shard_map/ppermute | solution.py:31
  76.8 0.0 collective-permute-start.9
  76.8 0.0 collective-permute-done.11.above_ref
  76.8 1.2 %local_part.1 = f32[3,8,8,2048]{3,2,1,0:T(8,128)S(1)} custom-call(f32[3,8,8,2048]{3,2,1,0:T(8,128)S(1)} %bitcast.16, f32[3,1,2048]{2,1,0:T(1,128)S(1)} %collective-permute-done.11.above_ref, f32[3,1,2048]{2,1,0:T(1,128)S(1)} %collective-permute-done.12.below_ref), custom_call_target="tpu_custom_call" | custom-call | tf_op jit(solution)/shard_map/local_part/pallas_call | solution.py:220
  78.0 0.0 copy-start.2
  78.0 0.2 collective-permute-done.10.far_ref
  78.2 3.6 %collective-permute-done.9.near_ref = f32[3,1,2048]{2,1,0:T(1,128)S(1)} collective-permute-done((f32[3,1,2048]{2,1,0:T(1,128)S(1)}, f32[3,1,2048]{2,1,0:T(1,128)S(1)}, u32[]{:S(2)}, u32[]{:S(2)}) %collective-permute-start.9) | collective-permute-done | bytes 24608 | tf_op jit(solution)/shard_map/ppermute | solution.py:31
  81.8 0.0 collective-permute-done.8.other_ref
  81.8 6.2 %coeffs.1 = f32[9,64,2048]{2,1,0:T(8,128)} custom-call(s32[2]{0:T(128)S(1)} %pad_add_fusion.where_ref, f32[3,4,8,2048]{3,2,1,0:T(8,128)} %get-tuple-element.12.half_ref, f32[3,4,8,2048]{3,2,1,0:T(8,128)} %collective-permute-done.8.other_ref, f32[3,1,2048]{2,1,0:T(1,128)S(1)} %collective-permute-done.9.near_ref, f32[3,1,2048]{2,1,0:T(1,128)S(1)} %collective-permute-done.10.far_ref), custom_call_target="tpu_custom_call" | custom-call | tf_op jit(solution)/shard_map/coeffs/pallas_call | solution.py:181
  88.0 0.0 collective-permute-done.14.refs_2_
  88.0 0.0 copy-done.2
  88.0 3.6 %residual.1 = f32[3,64,2048]{2,1,0:T(8,128)} custom-call(s32[1]{0:T(128)} %bitcast.6.which_ref, f32[3,64,2048]{2,1,0:T(8,128)S(1)} %bitcast.21, f32[3,64,2048]{2,1,0:T(8,128)S(1)} %collective-permute-done.refs_0_, f32[3,64,2048]{2,1,0:T(8,128)} %collective-permute-done.13.refs_1_, f32[3,64,2048]{2,1,0:T(8,128)} %collective-permute-done.14.refs_2_, ...), custom_call_target="tpu_custom_call" | custom-call | tf_op jit(solution)/shard_map/residual/pallas_call | solution.py:246
  (3 shorter events, 0.1 us)
Async XLA Ops:
  0.6 3.7 %collective-permute-start = (f32[3,64,2048]{2,1,0:T(8,128)}, f32[3,64,2048]{2,1,0:T(8,128)S(1)}, u32[]{:S(2)}, u32[]{:S(2)}) collective-permute-start(f32[3,64,2048]{2,1,0:T(8,128)} %bitcast.9), channel_id=1, source_target_pairs={{0,16},{16,0},{1,17},{17,1},{2,18},{18,2},{3,19},{19,3},{4,20},{20... | collective-permute-start | bytes 4718600 | tf_op jit(solution)/shard_map/ppermute | solution.py:31
  0.7 31.6 %collective-permute-start.13 = (f32[3,64,2048]{2,1,0:T(8,128)}, f32[3,64,2048]{2,1,0:T(8,128)}, u32[]{:S(2)}, u32[]{:S(2)}) collective-permute-start(f32[3,64,2048]{2,1,0:T(8,128)} %bitcast.10), channel_id=1, source_target_pairs={{16,32},{17,33},{18,34},{19,35},{20,36},{21,37},{22,38},{23,39},{2... | collective-permute-start | bytes 4718600 | tf_op jit(solution)/shard_map/ppermute | solution.py:31
  4.3 1.4 %copy-start = (f32[1,1,3,64,2048]{4,3,2,1,0:T(8,128)S(1)}, f32[1,1,3,64,2048]{4,3,2,1,0:T(8,128)}, u32[]{:S(2)}) copy-start(f32[1,1,3,64,2048]{4,3,2,1,0:T(8,128)} %param.2) | copy-start | bytes 4718596
  6.4 65.3 %copy-start.1 = (f32[1,1,3,64,2048]{4,3,2,1,0:T(8,128)S(1)}, f32[1,1,3,64,2048]{4,3,2,1,0:T(8,128)}, u32[]{:S(2)}) copy-start(f32[1,1,3,64,2048]{4,3,2,1,0:T(8,128)} %param.2) | copy-start | bytes 4718596
  6.4 19.6 %collective-permute-start.1 = (f32[3,8,2048]{2,1,0:T(8,128)S(1)}, f32[3,8,2048]{2,1,0:T(8,128)S(1)}, u32[]{:S(2)}, u32[]{:S(2)}) collective-permute-start(f32[3,8,2048]{2,1,0:T(8,128)S(1)} %get-tuple-element.9), channel_id=1, source_target_pairs={{0,64},{16,80},{1,65},{17,81},{2,66},{18,82},{3,67},{19,83},{4,68}... | collective-permute-start | bytes 589832 | tf_op jit(solution)/shard_map/ppermute | solution.py:31
  8.0 18.1 %collective-permute-start.2 = (f32[3,8,2048]{2,1,0:T(8,128)S(1)}, f32[3,8,2048]{2,1,0:T(8,128)S(1)}, u32[]{:S(2)}, u32[]{:S(2)}) collective-permute-start(f32[3,8,2048]{2,1,0:T(8,128)S(1)} %get-tuple-element.10), channel_id=1, source_target_pairs={{0,192},{16,208},{1,193},{17,209},{2,194},{18,210},{3,195},{19,211... | collective-permute-start | bytes 589832 | tf_op jit(solution)/shard_map/ppermute | solution.py:31
  8.5 17.5 %collective-permute-start.3 = (f32[3,8,2048]{2,1,0:T(8,128)S(1)}, f32[3,8,2048]{2,1,0:T(8,128)S(1)}, u32[]{:S(2)}, u32[]{:S(2)}) collective-permute-start(f32[3,8,2048]{2,1,0:T(8,128)S(1)} %get-tuple-element.11), channel_id=1, source_target_pairs={{0,128},{16,144},{1,129},{17,145},{2,130},{18,146},{3,131},{19,147... | collective-permute-start | bytes 589832 | tf_op jit(solution)/shard_map/ppermute | solution.py:31
  26.1 9.8 %collective-permute-start.4 = (f32[3,8,2048]{2,1,0:T(8,128)S(1)}, f32[3,8,2048]{2,1,0:T(8,128)S(1)}, u32[]{:S(2)}, u32[]{:S(2)}) collective-permute-start(f32[3,8,2048]{2,1,0:T(8,128)S(1)} %add_add_fusion), channel_id=1, source_target_pairs={{0,32},{16,48},{1,33},{17,49},{2,34},{18,50},{3,35},{19,51},{4,36}... | collective-permute-start | bytes 589832 | tf_op jit(solution)/shard_map/ppermute | solution.py:31
  32.3 55.7 %collective-permute-start.14 = (f32[3,64,2048]{2,1,0:T(8,128)}, f32[3,64,2048]{2,1,0:T(8,128)}, u32[]{:S(2)}, u32[]{:S(2)}) collective-permute-start(f32[3,64,2048]{2,1,0:T(8,128)} %collective-permute-done.13.refs_1_), channel_id=1, source_target_pairs={{252,8},{253,9},{254,10},{255,11}} | collective-permute-start | bytes 4718600 | tf_op jit(solution)/shard_map/ppermute | solution.py:31
  35.9 31.2 %collective-permute-start.7 = (f32[3,8,2048]{2,1,0:T(8,128)S(1)}, f32[3,8,2048]{2,1,0:T(8,128)S(1)}, u32[]{:S(2)}, u32[]{:S(2)}) collective-permute-start(f32[3,8,2048]{2,1,0:T(8,128)S(1)} %add_multiply_fusion.p0), channel_id=1, source_target_pairs={{0,64},{16,80},{1,65},{17,81},{2,66},{18,82},{3,67},{19,83},{4,68}... | collective-permute-start | bytes 589832 | tf_op jit(solution)/shard_map/ppermute | solution.py:31
  58.4 9.3 %collective-permute-start.6 = (f32[3,8,2048]{2,1,0:T(8,128)S(1)}, f32[3,8,2048]{2,1,0:T(8,128)S(1)}, u32[]{:S(2)}, u32[]{:S(2)}) collective-permute-start(f32[3,8,2048]{2,1,0:T(8,128)S(1)} %add_multiply_fusion.p0), channel_id=1, source_target_pairs={{0,128},{16,144},{1,129},{17,145},{2,130},{18,146},{3,131},{19,147... | collective-permute-start | bytes 589832 | tf_op jit(solution)/shard_map/ppermute | solution.py:31
  59.5 10.6 %collective-permute-start.5 = (f32[3,8,2048]{2,1,0:T(8,128)S(1)}, f32[3,8,2048]{2,1,0:T(8,128)S(1)}, u32[]{:S(2)}, u32[]{:S(2)}) collective-permute-start(f32[3,8,2048]{2,1,0:T(8,128)S(1)} %add_multiply_fusion.p0), channel_id=1, source_target_pairs={{0,192},{16,208},{1,193},{17,209},{2,194},{18,210},{3,195},{19,211... | collective-permute-start | bytes 589832 | tf_op jit(solution)/shard_map/ppermute | solution.py:31
  71.6 10.2 %collective-permute-start.8 = (f32[3,4,8,2048]{3,2,1,0:T(8,128)}, f32[3,4,8,2048]{3,2,1,0:T(8,128)}, u32[]{:S(2)}, u32[]{:S(2)}) collective-permute-start(f32[3,4,8,2048]{3,2,1,0:T(8,128)} %get-tuple-element.12.half_ref), channel_id=1, source_target_pairs={{0,16},{16,0},{1,17},{17,1},{2,18},{18,2},{3,19},{19,3},{4,20},{20... | collective-permute-start | bytes 2359304 | tf_op jit(solution)/shard_map/ppermute | solution.py:31
  71.7 5.1 %collective-permute-start.12 = (f32[3,1,2048]{2,1,0:T(1,128)S(1)}, f32[3,1,2048]{2,1,0:T(1,128)S(1)}, u32[]{:S(2)}, u32[]{:S(2)}) collective-permute-start(f32[3,1,2048]{2,1,0:T(1,128)S(1)} %get-tuple-element.14), channel_id=1, source_target_pairs={{0,3},{16,19},{1,0},{17,16},{2,1},{18,17},{3,2},{19,18},{4,7},{20,... | collective-permute-start | bytes 73736 | tf_op jit(solution)/shard_map/ppermute | solution.py:31
  72.5 4.3 %collective-permute-start.11 = (f32[3,1,2048]{2,1,0:T(1,128)S(1)}, f32[3,1,2048]{2,1,0:T(1,128)S(1)}, u32[]{:S(2)}, u32[]{:S(2)}) collective-permute-start(f32[3,1,2048]{2,1,0:T(1,128)S(1)} %get-tuple-element.15), channel_id=1, source_target_pairs={{0,1},{16,17},{1,2},{17,18},{2,3},{18,19},{3,0},{19,16},{4,5},{20,... | collective-permute-start | bytes 73736 | tf_op jit(solution)/shard_map/ppermute | solution.py:31
  75.0 3.3 %collective-permute-start.10 = (f32[3,1,2048]{2,1,0:T(1,128)S(1)}, f32[3,1,2048]{2,1,0:T(1,128)S(1)}, u32[]{:S(2)}, u32[]{:S(2)}) collective-permute-start(f32[3,1,2048]{2,1,0:T(1,128)S(1)} %get-tuple-element.13), channel_id=1, source_target_pairs={{0,19},{16,1},{1,16},{17,2},{2,17},{18,3},{3,18},{19,0},{4,23},{20... | collective-permute-start | bytes 73736 | tf_op jit(solution)/shard_map/ppermute | solution.py:31
  76.8 5.0 %collective-permute-start.9 = (f32[3,1,2048]{2,1,0:T(1,128)S(1)}, f32[3,1,2048]{2,1,0:T(1,128)S(1)}, u32[]{:S(2)}, u32[]{:S(2)}) collective-permute-start(f32[3,1,2048]{2,1,0:T(1,128)S(1)} %get-tuple-element.13), channel_id=1, source_target_pairs={{0,3},{16,17},{1,0},{17,18},{2,1},{18,19},{3,2},{19,16},{4,7},{20,... | collective-permute-start | bytes 73736 | tf_op jit(solution)/shard_map/ppermute | solution.py:31
  78.0 10.0 %copy-start.2 = (f32[3,64,2048]{2,1,0:T(8,128)S(1)}, f32[3,64,2048]{2,1,0:T(8,128)}, u32[]{:S(2)}) copy-start(f32[3,64,2048]{2,1,0:T(8,128)} %refs_3_.1) | copy-start | bytes 4718596

commit v2 on v1

v2 whole, which is shorter than its diff:
```python
import jax
import jax.numpy as jnp
from jax import lax
from jax.experimental import pallas as pl
from jax.experimental.pallas import tpu as pltpu
from jax.sharding import PartitionSpec as P

AXES = ("tm", "win", "space")
VMEM_BYTES = 12 * 1024 * 1024
WHOLE = pl.BlockSpec(memory_space=pltpu.VMEM)
SCALARS = pl.BlockSpec(memory_space=pltpu.SMEM)


def place(x, z, y, core):
    z_hi, z_lo = divmod(z % 8, 4)
    tm = ((x % 4) * 2 + z_hi) * 2 + core
    return (tm * 4 + z_lo) * 4 + y % 4


def pairs(target):
    found = []
    for x in range(4):
        for z in range(8):
            for y in range(4):
                for core in range(2):
                    to = target(x, z, y, core)
                    if to is not None:
                        found.append((place(x, z, y, core), place(*to)))
    return found


def send(value, target):
    return lax.ppermute(value, AXES, pairs(target))


def cross_first(x, z, y, core):
    if core == 0 or (x, z) == (3, 7):
        return None
    return (x, z + 4, y, 0) if z < 4 else (x, z - 4, y, 1)


def step_last(x, z, y, core):
    if core == 0 or z > 3:
        return None
    if x < 3:
        return (x + 1, z, y, 0)
    return (0, z + 1, y, 0) if z < 3 else None


def step_first(x, z, y, core):
    if core == 0 or z < 4:
        return None
    if x < 3:
        return (x + 1, z, y, 1)
    return (0, z + 1, y, 1) if z < 7 else None


def cross_last(x, z, y, core):
    return (x, z + 4, y, 0) if core == 1 else None


def swap_target(x, z, y, core):
    return (x, z, y, 1 - core)


def after(value, *others):
    return lax.optimization_barrier((value,) + others)[0]


def x_target(by):
    return lambda x, z, y, core: (x + by, z, y, core)


def z_target(x, z, y, core):
    return (x, z + 4, y, core)


def up_target(x, z, y, core):
    return (x, z, y + 1, core)


def down_target(x, z, y, core):
    return (x, z, y - 1, core)


def edge_target(flip):
    def target(x, z, y, core):
        return (x, z, y - 1 if core == 0 else y + 1, core ^ flip)

    return target


def call(kernel, out_shape, *operands, **options):
    return pl.pallas_call(
        kernel,
        out_shape=out_shape,
        compiler_params=pltpu.CompilerParams(vmem_limit_bytes=VMEM_BYTES),
        cost_estimate=pl.CostEstimate(flops=1, bytes_accessed=1, transcendentals=0),
        **options,
    )(*operands)


def in_vmem(value):
    return pltpu.with_memory_space_constraint(value, pltpu.VMEM)


def vmem_out(*shape):
    return pltpu.VMEM(shape, jnp.float32)


def ddx(value):
    width = value.shape[1]
    return (pltpu.roll(value, width - 1, 1) - pltpu.roll(value, 1, 1)) * 0.5


def ddy(above, value, below):
    row = lax.broadcasted_iota(jnp.int32, value.shape, 0)
    after = jnp.where(row == 7, pltpu.roll(below, 7, 0), pltpu.roll(value, 7, 0))
    before = jnp.where(row == 0, pltpu.roll(above, 1, 0), pltpu.roll(value, 1, 0))
    return (after - before) * 0.5


def split_kernel(where_ref, own_ref, other_ref, *out_refs):
    x, core = where_ref[0], where_ref[1]
    for k, out_ref in enumerate(out_refs):
        block = core * 4 + (x + k) % 4
        out_ref[...] = own_ref[:, block] + other_ref[:, block]


def split_sum(where, own, other):
    cols = own.shape[-1]
    own, other = (a.reshape(3, 8, 8, cols) for a in (own, other))
    return call(
        split_kernel,
        [vmem_out(3, 8, cols)] * 4,
        where,
        in_vmem(own),
        in_vmem(other),
        in_specs=[SCALARS, WHOLE, WHOLE],
        out_specs=[WHOLE] * 4,
        name="split_sum",
    )


def edge_kernel(where_ref, p0, p1, p2, p3, edge_ref):
    x, core = where_ref[0], where_ref[1]
    for k, piece in enumerate((p0, p1, p2, p3)):
        slot = (x + k) % 4

        @pl.when((core == 0) & (slot == 0))
        def _():
            edge_ref[...] = piece[:, 0:1]

        @pl.when((core == 1) & (slot == 3))
        def _():
            edge_ref[...] = piece[:, 7:8]


def edge_of(where, pieces):
    cols = pieces[0].shape[-1]
    return call(
        edge_kernel,
        vmem_out(3, 1, cols),
        where,
        *map(in_vmem, pieces),
        in_specs=[SCALARS] + [WHOLE] * 4,
        out_specs=WHOLE,
        name="edge",
    )


def coeffs_kernel(where_ref, *refs):
    near_ref, far_ref, out_ref, mean, fields, sems = refs[8:]
    x, core = where_ref[0], where_ref[1]
    for k in range(4):
        slot = (x + k) % 4
        mean[:, 1 + core * 4 + slot] = refs[k][...]
        mean[:, 5 - core * 4 + slot] = refs[4 + k][...]

    @pl.when(core == 0)
    def _():
        mean[:, 9, 0:1] = near_ref[...]
        mean[:, 0, 7:8] = far_ref[...]

    @pl.when(core == 1)
    def _():
        mean[:, 0, 7:8] = near_ref[...]
        mean[:, 9, 0:1] = far_ref[...]

    copies = []
    for part in range(4):
        rows = pl.ds(part * 16, 16)
        for f in range(3):
            for r in (2 * part, 2 * part + 1):
                value = mean[f, r + 1]
                block = pl.ds(r * 8, 8)
                fields[f, block] = value + 1.0 if f == 2 else value
                fields[3 + 2 * f, block] = ddx(value)
                fields[4 + 2 * f, block] = ddy(mean[f, r], value, mean[f, r + 2])
            for planes in (pl.ds(f, 1), pl.ds(3 + 2 * f, 2)):
                copy = pltpu.make_async_copy(fields.at[planes, rows], out_ref.at[planes, rows], sems.at[len(copies)])
                copy.start()
                copies.append(copy)
    for copy in copies:
        copy.wait()


def coeffs_of(where, pieces, others, near, far):
    cols = near.shape[-1]
    return call(
        coeffs_kernel,
        jax.ShapeDtypeStruct((9, 64, cols), jnp.float32),
        where,
        *map(in_vmem, (*pieces, *others, near, far)),
        in_specs=[SCALARS] + [WHOLE] * 10,
        out_specs=pl.BlockSpec(memory_space=pl.ANY),
        scratch_shapes=[
            pltpu.VMEM((3, 10, 8, cols), jnp.float32),
            pltpu.VMEM((9, 64, cols), jnp.float32),
            pltpu.SemaphoreType.DMA((24,)),
        ],
        name="coeffs",
    )


def stage_kernel(state_ref, out_ref):
    out_ref[...] = state_ref[...]


def stage(state):
    return call(stage_kernel, vmem_out(*state.shape), state, in_specs=[WHOLE], out_specs=WHOLE, name="stage")


def local_kernel(which_ref, state_ref, above_ref, below_ref, other_ref, initial_ref, out_ref):
    def block(f, r):
        if r < 0:
            return jnp.broadcast_to(above_ref[f], (8, above_ref.shape[-1]))
        if r > 7:
            return jnp.broadcast_to(below_ref[f], (8, below_ref.shape[-1]))
        return state_ref[f, r]

    for r in range(8):
        u, v, e = (state_ref[f, r] for f in range(3))
        dx = [ddx(w) for w in (u, v, e)]
        dy = [ddy(block(f, r - 1), w, block(f, r + 1)) for f, w in enumerate((u, v, e))]
        force_u = -u * dx[0] - v * dy[0] + v - dx[2]
        force_v = -u * dx[1] - v * dy[1] - u - dy[2]
        depth = 1.0 + e
        force_e = -(depth * dx[0] + u * dx[2]) - (depth * dy[1] + v * dy[2])
        out_ref[0, r] = u - 0.5 * force_u
        out_ref[1, r] = v - 0.5 * force_v
        out_ref[2, r] = e - 0.5 * force_e

    @pl.when(which_ref[0] == 1)
    def _():
        out_ref[...] = out_ref[...] - other_ref[...]

    @pl.when(which_ref[0] == 2)
    def _():
        out_ref[...] = out_ref[...] - initial_ref[...]


def local_part(which, state, above, below, other, initial):
    cols = state.shape[-1]
    state, other, initial = (a.reshape(3, 8, 8, cols) for a in (state, other, initial))
    return call(
        local_kernel,
        vmem_out(3, 8, 8, cols),
        which,
        *map(in_vmem, (state, above, below, other, initial)),
        in_specs=[SCALARS] + [WHOLE] * 5,
        out_specs=WHOLE,
        name="local_part",
    ).reshape(3, 64, cols)


def residual_kernel(core_ref, local_ref, crossed_ref, stepped_ref, second_ref, out_ref, left, sems):
    first, second = slice(0, 32), slice(32, 64)
    left[:, first] = local_ref[:, first] - stepped_ref[...]

    @pl.when(core_ref[0] == 0)
    def _():
        left[:, first] = left[:, first] - crossed_ref[...]

    copies = [pltpu.make_async_copy(left.at[:, first], out_ref.at[:, first], sems.at[0])]
    copies[0].start()
    left[:, second] = local_ref[:, second] - second_ref[...]
    copies.append(pltpu.make_async_copy(left.at[:, second], out_ref.at[:, second], sems.at[1]))
    copies[1].start()
    for copy in copies:
        copy.wait()


def residual_of(core, local, crossed, stepped, second):
    return call(
        residual_kernel,
        jax.ShapeDtypeStruct(local.shape, jnp.float32),
        core,
        *map(in_vmem, (local, crossed, stepped, second)),
        in_specs=[SCALARS] + [WHOLE] * 4,
        out_specs=pl.BlockSpec(memory_space=pl.ANY),
        scratch_shapes=[pltpu.VMEM(local.shape, jnp.float32), pltpu.SemaphoreType.DMA((2,))],
        name="residual",
    )


def shards(states, initial_state):
    current = states[0, 0]
    step, window = lax.axis_index("tm"), lax.axis_index("win")
    x, z_hi, core = step // 4, step // 2 % 2, step % 2
    where = jnp.stack([x, core]).astype(jnp.int32)

    other = send(current, swap_target)
    crossed = send(current[:, :32], cross_first)
    held = stage(current)

    pieces = split_sum(where, held, other)
    above = send(after(held, pieces[0])[:, 63:64], up_target)
    below = send(after(held, pieces[0])[:, 0:1], down_target)
    came = [send(pieces[k], x_target(k)) for k in (1, 3, 2)]
    part = (pieces[0] + came[0]) + (came[1] + came[2])

    second_half = after(held, part)[:, 32:]
    shifted = send(second_half, step_first)
    stepped = send(after(crossed, part), step_last)
    which = jnp.where(core == 1, 1, jnp.where((step == 0) & (window == 0), 2, 0)).astype(jnp.int32).reshape(1)
    local = local_part(which, after(held, part), above, below, other, initial_state)

    part = (part + after(send(part, z_target), crossed, shifted, local)) * (1.0 / 16.0)
    second = send(after(jnp.where(z_hi == 0, second_half, shifted), part), cross_last)
    gathered = [part] + [send(part, x_target(-k)) for k in (1, 2, 3)]
    others = [send(piece, swap_target) for piece in gathered]
    edge = edge_of(where, gathered)
    near = send(edge, edge_target(0))
    beyond = send(edge, edge_target(1))
    coeffs = coeffs_of(where, gathered, others, near, beyond)

    local = after(local, coeffs)
    residual = residual_of(core.astype(jnp.int32).reshape(1), local, crossed, stepped, second)
    return coeffs[None], residual[None, None]


def solution(mesh):
    in_specs = (P("win", "tm", None, "space", None), P(None, "space", None))
    out_specs = (P("win", None, "space", None), P("win", "tm", None, "space", None))
    return jax.shard_map(shards, mesh=mesh, in_specs=in_specs, out_specs=out_specs, check_vma=False)
```

time: 91.8 us -> 79.2 us (0.86)
  the two profiles are of different devices: /device:TPU:26 before, /device:TPU:33 now
where the time goes in v2:
time: 79.2 us; the launch traced here: 78.9 us
  starting transfers between devices  42.4 us (54%)
  waiting for transfers between devices  21.6 us (27%)
  Pallas kernels  8.21 us (10%)
  local copies, waits for them, and re-layouts  4.72 us (6%)
  other arithmetic  1.17 us (1%)
  between operations  0.83 us (1%)
    ppermute x20, starting transfers between devices, send(): return lax.ppermute(value, AXES, pairs(target))  42.4 us
    ppermute x20, waiting for transfers between devices, send(): return lax.ppermute(value, AXES, pairs(target))  21.6 us
    pallas_call x6, Pallas kernels, call(): pl.pallas_call(kernel, out_shape=out_shape, compiler_params=pltpu.Compile...  8.21 us
    unnamed x6, local copies, waits for them, and re-layouts  2.81 us
  transfers between devices with their start and end apart: 20, of which 7 were waited for; matrix products, arithmetic and copies ran while one was open for 4% of the time, Pallas kernels for 7%

profile of v2, /device:TPU:33, one launch (start us, length us, event | category | flops | bytes accessed | tf_op | source)
XLA Modules:
  0.0 78.9 jit_solution(14146971524608738967)
XLA Ops:
  0.6 0.8 collective-permute-start
  1.4 0.0 copy-start
  1.4 1.4 %copy-done = f32[1,1,3,64,2048]{4,3,2,1,0:T(8,128)S(1)} copy-done((f32[1,1,3,64,2048]{4,3,2,1,0:T(8,128)S(1)}, f32[1,1,3,64,2048]{4,3,2,1,0:T(8,128)}, u32[]{:S(2)}) %copy-start) | copy-done | bytes 1572888
  2.8 0.1 stage.1
  2.9 0.1 pad_add_fusion.where_ref
  3.0 1.6 %collective-permute-done = f32[3,64,2048]{2,1,0:T(8,128)S(1)} collective-permute-done((f32[3,64,2048]{2,1,0:T(8,128)}, f32[3,64,2048]{2,1,0:T(8,128)S(1)}, u32[]{:S(2)}, u32[]{:S(2)}) %collective-permute-start) | collective-permute-done | bytes 1572896 | tf_op jit(solution)/shard_map/ppermute | solution.py:33
  4.6 0.0 copy-start.1
  4.6 0.6 split_sum.1
  5.3 1.3 %collective-permute-start.1 = (f32[3,8,2048]{2,1,0:T(8,128)S(1)}, f32[3,8,2048]{2,1,0:T(8,128)S(1)}, u32[]{:S(2)}, u32[]{:S(2)}) collective-permute-start(f32[3,8,2048]{2,1,0:T(8,128)S(1)} %get-tuple-element.13), channel_id=1, source_target_pairs={{0,64},{16,80},{1,65},{17,81},{2,66},{18,82},{3,67},{19,83},{4,68}... | collective-permute-start | bytes 589832 | tf_op jit(solution)/shard_map/ppermute | solution.py:33
  6.6 1.5 %collective-permute-start.2 = (f32[3,8,2048]{2,1,0:T(8,128)S(1)}, f32[3,8,2048]{2,1,0:T(8,128)S(1)}, u32[]{:S(2)}, u32[]{:S(2)}) collective-permute-start(f32[3,8,2048]{2,1,0:T(8,128)S(1)} %get-tuple-element.14), channel_id=1, source_target_pairs={{0,192},{16,208},{1,193},{17,209},{2,194},{18,210},{3,195},{19,211... | collective-permute-start | bytes 589832 | tf_op jit(solution)/shard_map/ppermute | solution.py:33
  8.0 1.5 %collective-permute-start.3 = (f32[3,8,2048]{2,1,0:T(8,128)S(1)}, f32[3,8,2048]{2,1,0:T(8,128)S(1)}, u32[]{:S(2)}, u32[]{:S(2)}) collective-permute-start(f32[3,8,2048]{2,1,0:T(8,128)S(1)} %get-tuple-element.15), channel_id=1, source_target_pairs={{0,128},{16,144},{1,129},{17,145},{2,130},{18,146},{3,131},{19,147... | collective-permute-start | bytes 589832 | tf_op jit(solution)/shard_map/ppermute | solution.py:33
  9.6 0.0 copy-done.1
  9.6 0.9 %slice.16 = f32[3,32,2048]{2,1,0:T(8,128)} slice(f32[3,64,2048]{2,1,0:T(8,128)S(1)} %bitcast.18), slice={[0:3], [0:32], [0:2048]} | slice | bytes 1572864 | tf_op jit(solution)/shard_map/slice | solution.py:314
  10.5 9.0 %collective-permute-start.5 = (f32[3,32,2048]{2,1,0:T(8,128)}, f32[3,32,2048]{2,1,0:T(8,128)}, u32[]{:S(2)}, u32[]{:S(2)}) collective-permute-start(f32[3,32,2048]{2,1,0:T(8,128)} %slice.16), channel_id=1, source_target_pairs={{16,32},{17,33},{18,34},{19,35},{20,36},{21,37},{22,38},{23,39},{2... | collective-permute-start | bytes 2359304 | tf_op jit(solution)/shard_map/ppermute | solution.py:33
  19.5 0.0 collective-permute-done.1
  19.5 0.0 collective-permute-done.2
  19.5 0.0 collective-permute-done.3
  19.6 0.9 %slice.13 = f32[3,32,2048]{2,1,0:T(8,128)} slice(f32[3,64,2048]{2,1,0:T(8,128)S(1)} %stage.1), slice={[0:3], [32:64], [0:2048]} | slice | bytes 1572864 | tf_op jit(solution)/shard_map/slice | solution.py:323
  20.5 1.6 %collective-permute-start.6 = (f32[3,32,2048]{2,1,0:T(8,128)}, f32[3,32,2048]{2,1,0:T(8,128)}, u32[]{:S(2)}, u32[]{:S(2)}) collective-permute-start(f32[3,32,2048]{2,1,0:T(8,128)} %slice.13), channel_id=1, source_target_pairs={{48,112},{49,113},{50,114},{51,115},{52,116},{53,117},{54,118},{55... | collective-permute-start | bytes 2359304 | tf_op jit(solution)/shard_map/ppermute | solution.py:33
  22.1 5.3 %collective-permute-start.4 = (f32[3,8,2048]{2,1,0:T(8,128)S(1)}, f32[3,8,2048]{2,1,0:T(8,128)}, u32[]{:S(2)}, u32[]{:S(2)}) collective-permute-start(f32[3,8,2048]{2,1,0:T(8,128)S(1)} %add_add_fusion), channel_id=1, source_target_pairs={{0,32},{16,48},{1,33},{17,49},{2,34},{18,50},{3,35},{19,51},{4,36}... | collective-permute-start | bytes 589832 | tf_op jit(solution)/shard_map/ppermute | solution.py:33
  27.4 1.4 %collective-permute-start.7 = (f32[3,1,2048]{2,1,0:T(1,128)S(1)}, f32[3,1,2048]{2,1,0:T(1,128)S(1)}, u32[]{:S(2)}, u32[]{:S(2)}) collective-permute-start(f32[3,1,2048]{2,1,0:T(1,128)S(1)} %get-tuple-element.23), channel_id=1, source_target_pairs={{0,1},{16,17},{1,2},{17,18},{2,3},{18,19},{3,0},{19,16},{4,5},{20,... | collective-permute-start | bytes 73736 | tf_op jit(solution)/shard_map/ppermute | solution.py:33
  28.8 1.5 %collective-permute-start.8 = (f32[3,1,2048]{2,1,0:T(1,128)S(1)}, f32[3,1,2048]{2,1,0:T(1,128)S(1)}, u32[]{:S(2)}, u32[]{:S(2)}) collective-permute-start(f32[3,1,2048]{2,1,0:T(1,128)S(1)} %get-tuple-element.22), channel_id=1, source_target_pairs={{0,3},{16,19},{1,0},{17,16},{2,1},{18,17},{3,2},{19,18},{4,7},{20,... | collective-permute-start | bytes 73736 | tf_op jit(solution)/shard_map/ppermute | solution.py:33
  30.3 13.0 %collective-permute-done.5.crossed_ref = f32[3,32,2048]{2,1,0:T(8,128)} collective-permute-done((f32[3,32,2048]{2,1,0:T(8,128)}, f32[3,32,2048]{2,1,0:T(8,128)}, u32[]{:S(2)}, u32[]{:S(2)}) %collective-permute-start.5) | collective-permute-done | bytes 786464 | tf_op jit(solution)/shard_map/ppermute | solution.py:33
  43.3 1.3 %collective-permute-start.18 = (f32[3,32,2048]{2,1,0:T(8,128)}, f32[3,32,2048]{2,1,0:T(8,128)S(1)}, u32[]{:S(2)}, u32[]{:S(2)}) collective-permute-start(f32[3,32,2048]{2,1,0:T(8,128)} %collective-permute-done.5.crossed_ref), channel_id=1, source_target_pairs={{16,64},{17,65},{18,66},{19,67},{20,68},{21,69},{22,70},{23,71},{2... | collective-permute-start | bytes 2359304 | tf_op jit(solution)/shard_map/ppermute | solution.py:33
  44.6 0.0 collective-permute-done.7.above_ref
  44.6 0.0 collective-permute-done.8.below_ref
  44.7 0.0 copy-start.2
  44.7 1.4 %copy-done.2 = f32[3,64,2048]{2,1,0:T(8,128)S(1)} copy-done((f32[3,64,2048]{2,1,0:T(8,128)S(1)}, f32[3,64,2048]{2,1,0:T(8,128)}, u32[]{:S(2)}) %copy-start.2) | copy-done | bytes 1572888
  46.1 1.3 %local_part.1 = f32[3,8,8,2048]{3,2,1,0:T(8,128)S(1)} custom-call(s32[1]{0:T(128)} %bitcast.5.which_ref, f32[3,8,8,2048]{3,2,1,0:T(8,128)S(1)} %bitcast.12, f32[3,1,2048]{2,1,0:T(1,128)S(1)} %collective-permute-done.7.above_ref, f32[3,1,2048]{2,1,0:T(1,128)S(1)} %collective-permute-done.8.below_ref, f32[3,8,8,2048]{3,2,1,0:T(8,128)S(1)} %bitcast.14, ...), custom_call_target="tpu_custom_call" | custom-call | flops 1 | bytes 1 | tf_op jit(solution)/shard_map/local_part/pallas_call | solution.py:94
  47.4 0.0 collective-permute-done.4
  47.4 0.0 collective-permute-done.6
  47.4 1.0 %add_multiply_fusion.p0.refs_0_ = f32[3,8,2048]{2,1,0:T(8,128)S(1)} fusion(f32[3,8,2048]{2,1,0:T(8,128)S(1)} %add_add_fusion, f32[3,8,2048]{2,1,0:T(8,128)} %collective-permute-done.4), kind=kLoop, calls=%fused_computation.1 | loop fusion | flops 98304 | bytes 589824 | tf_op jit(solution)/shard_map/mul | solution.py:329
  48.4 0.1 broadcast_select_fusion
  48.5 8.7 %collective-permute-start.19 = (f32[3,32,2048]{2,1,0:T(8,128)S(1)}, f32[3,32,2048]{2,1,0:T(8,128)S(1)}, u32[]{:S(2)}, u32[]{:S(2)}) collective-permute-start(f32[3,32,2048]{2,1,0:T(8,128)S(1)} %broadcast_select_fusion), channel_id=1, source_target_pairs={{16,32},{17,33},{18,34},{19,35},{20,36},{21,37},{22,38},{23,39},{2... | collective-permute-start | bytes 2359304 | tf_op jit(solution)/shard_map/ppermute | solution.py:33
  57.2 1.5 %collective-permute-start.10 = (f32[3,8,2048]{2,1,0:T(8,128)S(1)}, f32[3,8,2048]{2,1,0:T(8,128)S(1)}, u32[]{:S(2)}, u32[]{:S(2)}) collective-permute-start(f32[3,8,2048]{2,1,0:T(8,128)S(1)} %add_multiply_fusion.p0.refs_0_), channel_id=1, source_target_pairs={{0,128},{16,144},{1,129},{17,145},{2,130},{18,146},{3,131},{19,147... | collective-permute-start | bytes 589832 | tf_op jit(solution)/shard_map/ppermute | solution.py:33
  58.7 0.0 collective-permute-start.11
  58.7 2.7 %collective-permute-start.9 = (f32[3,8,2048]{2,1,0:T(8,128)S(1)}, f32[3,8,2048]{2,1,0:T(8,128)S(1)}, u32[]{:S(2)}, u32[]{:S(2)}) collective-permute-start(f32[3,8,2048]{2,1,0:T(8,128)S(1)} %add_multiply_fusion.p0.refs_0_), channel_id=1, source_target_pairs={{0,192},{16,208},{1,193},{17,209},{2,194},{18,210},{3,195},{19,211... | collective-permute-start | bytes 589832 | tf_op jit(solution)/shard_map/ppermute | solution.py:33
  61.4 2.2 %collective-permute-done.10.p2.refs_2_ = f32[3,8,2048]{2,1,0:T(8,128)S(1)} collective-permute-done((f32[3,8,2048]{2,1,0:T(8,128)S(1)}, f32[3,8,2048]{2,1,0:T(8,128)S(1)}, u32[]{:S(2)}, u32[]{:S(2)}) %collective-permute-start.10) | collective-permute-done | bytes 196640 | tf_op jit(solution)/shard_map/ppermute | solution.py:33
  63.6 0.0 collective-permute-start.12
  63.6 2.1 %collective-permute-done.11.p3.refs_3_ = f32[3,8,2048]{2,1,0:T(8,128)S(1)} collective-permute-done((f32[3,8,2048]{2,1,0:T(8,128)S(1)}, f32[3,8,2048]{2,1,0:T(8,128)S(1)}, u32[]{:S(2)}, u32[]{:S(2)}) %collective-permute-start.11) | collective-permute-done | bytes 196640 | tf_op jit(solution)/shard_map/ppermute | solution.py:33
  65.7 0.0 collective-permute-done.9.p1.refs_1_
  65.7 0.6 edge.1
  66.3 1.4 %collective-permute-start.16 = (f32[3,1,2048]{2,1,0:T(1,128)S(1)}, f32[3,1,2048]{2,1,0:T(1,128)S(1)}, u32[]{:S(2)}, u32[]{:S(2)}) collective-permute-start(f32[3,1,2048]{2,1,0:T(1,128)S(1)} %edge.1), channel_id=1, source_target_pairs={{0,3},{16,17},{1,0},{17,18},{2,1},{18,19},{3,2},{19,16},{4,7},{20,... | collective-permute-start | bytes 73736 | tf_op jit(solution)/shard_map/ppermute | solution.py:33
  67.7 0.0 collective-permute-start.17
  67.7 0.0 collective-permute-done.12.refs_4_
  67.7 1.9 %collective-permute-start.13 = (f32[3,8,2048]{2,1,0:T(8,128)S(1)}, f32[3,8,2048]{2,1,0:T(8,128)S(1)}, u32[]{:S(2)}, u32[]{:S(2)}) collective-permute-start(f32[3,8,2048]{2,1,0:T(8,128)S(1)} %collective-permute-done.9.p1.refs_1_), channel_id=1, source_target_pairs={{0,16},{16,0},{1,17},{17,1},{2,18},{18,2},{3,19},{19,3},{4,20},{20... | collective-permute-start | bytes 589832 | tf_op jit(solution)/shard_map/ppermute | solution.py:33
  69.6 1.0 %collective-permute-done.16.refs_8_ = f32[3,1,2048]{2,1,0:T(1,128)S(1)} collective-permute-done((f32[3,1,2048]{2,1,0:T(1,128)S(1)}, f32[3,1,2048]{2,1,0:T(1,128)S(1)}, u32[]{:S(2)}, u32[]{:S(2)}) %collective-permute-start.16) | collective-permute-done | bytes 24608 | tf_op jit(solution)/shard_map/ppermute | solution.py:33
  70.6 0.0 collective-permute-start.14
  70.6 0.6 collective-permute-done.17.refs_9_
  71.2 1.0 %collective-permute-start.15 = (f32[3,8,2048]{2,1,0:T(8,128)S(1)}, f32[3,8,2048]{2,1,0:T(8,128)S(1)}, u32[]{:S(2)}, u32[]{:S(2)}) collective-permute-start(f32[3,8,2048]{2,1,0:T(8,128)S(1)} %collective-permute-done.11.p3.refs_3_), channel_id=1, source_target_pairs={{0,16},{16,0},{1,17},{17,1},{2,18},{18,2},{3,19},{19,3},{4,20},{20... | collective-permute-start | bytes 589832 | tf_op jit(solution)/shard_map/ppermute | solution.py:33
  72.3 0.0 collective-permute-done.13.refs_5_
  72.3 0.0 collective-permute-done.14.refs_6_
  72.3 1.1 %collective-permute-done.15.refs_7_ = f32[3,8,2048]{2,1,0:T(8,128)S(1)} collective-permute-done((f32[3,8,2048]{2,1,0:T(8,128)S(1)}, f32[3,8,2048]{2,1,0:T(8,128)S(1)}, u32[]{:S(2)}, u32[]{:S(2)}) %collective-permute-start.15) | collective-permute-done | bytes 196640 | tf_op jit(solution)/shard_map/ppermute | solution.py:33
  73.4 3.2 %coeffs.1 = f32[9,64,2048]{2,1,0:T(8,128)} custom-call(s32[2]{0:T(128)S(1)} %pad_add_fusion.where_ref, f32[3,8,2048]{2,1,0:T(8,128)S(1)} %add_multiply_fusion.p0.refs_0_, f32[3,8,2048]{2,1,0:T(8,128)S(1)} %collective-permute-done.9.p1.refs_1_, f32[3,8,2048]{2,1,0:T(8,128)S(1)} %collective-permute-done.10.p2.refs_2_, ...), custom_call_target="tpu_custom_call" | custom-call | flops 1 | bytes 1 | tf_op jit(solution)/shard_map/coeffs/pallas_call | solution.py:94
  76.5 0.0 collective-permute-done.18.stepped_ref
  76.5 0.0 collective-permute-done.19.second_ref
  76.6 2.4 %residual.1 = f32[3,64,2048]{2,1,0:T(8,128)} custom-call(s32[1]{0:T(128)} %bitcast.1.core_ref, f32[3,64,2048]{2,1,0:T(8,128)S(1)} %bitcast.15, f32[3,32,2048]{2,1,0:T(8,128)} %collective-permute-done.5.crossed_ref, f32[3,32,2048]{2,1,0:T(8,128)S(1)} %collective-permute-done.18.stepped_ref, f32[3,32,2048]{2,1,0:T(8,128)S(1)} %collective-permute-done.19.second_ref), custom_call_target="tpu_custom_call" | custom-call | flops 1 | bytes 1 | tf_op jit(solution)/shard_map/residual/pallas_call | solution.py:94
  (2 shorter events, 0.1 us)
Async XLA Ops:
  0.6 4.0 %collective-permute-start = (f32[3,64,2048]{2,1,0:T(8,128)}, f32[3,64,2048]{2,1,0:T(8,128)S(1)}, u32[]{:S(2)}, u32[]{:S(2)}) collective-permute-start(f32[3,64,2048]{2,1,0:T(8,128)} %bitcast.16), channel_id=1, source_target_pairs={{0,16},{16,0},{1,17},{17,1},{2,18},{18,2},{3,19},{19,3},{4,20},{20... | collective-permute-start | bytes 4718600 | tf_op jit(solution)/shard_map/ppermute | solution.py:33
  1.4 1.4 %copy-start = (f32[1,1,3,64,2048]{4,3,2,1,0:T(8,128)S(1)}, f32[1,1,3,64,2048]{4,3,2,1,0:T(8,128)}, u32[]{:S(2)}) copy-start(f32[1,1,3,64,2048]{4,3,2,1,0:T(8,128)} %param.2) | copy-start | bytes 4718596
  4.6 4.9 %copy-start.1 = (f32[1,1,3,64,2048]{4,3,2,1,0:T(8,128)S(1)}, f32[1,1,3,64,2048]{4,3,2,1,0:T(8,128)}, u32[]{:S(2)}) copy-start(f32[1,1,3,64,2048]{4,3,2,1,0:T(8,128)} %param.2) | copy-start | bytes 4718596
  5.3 14.2 %collective-permute-start.1 = (f32[3,8,2048]{2,1,0:T(8,128)S(1)}, f32[3,8,2048]{2,1,0:T(8,128)S(1)}, u32[]{:S(2)}, u32[]{:S(2)}) collective-permute-start(f32[3,8,2048]{2,1,0:T(8,128)S(1)} %get-tuple-element.13), channel_id=1, source_target_pairs={{0,64},{16,80},{1,65},{17,81},{2,66},{18,82},{3,67},{19,83},{4,68}... | collective-permute-start | bytes 589832 | tf_op jit(solution)/shard_map/ppermute | solution.py:33
  6.6 13.0 %collective-permute-start.2 = (f32[3,8,2048]{2,1,0:T(8,128)S(1)}, f32[3,8,2048]{2,1,0:T(8,128)S(1)}, u32[]{:S(2)}, u32[]{:S(2)}) collective-permute-start(f32[3,8,2048]{2,1,0:T(8,128)S(1)} %get-tuple-element.14), channel_id=1, source_target_pairs={{0,192},{16,208},{1,193},{17,209},{2,194},{18,210},{3,195},{19,211... | collective-permute-start | bytes 589832 | tf_op jit(solution)/shard_map/ppermute | solution.py:33
  8.0 11.5 %collective-permute-start.3 = (f32[3,8,2048]{2,1,0:T(8,128)S(1)}, f32[3,8,2048]{2,1,0:T(8,128)S(1)}, u32[]{:S(2)}, u32[]{:S(2)}) collective-permute-start(f32[3,8,2048]{2,1,0:T(8,128)S(1)} %get-tuple-element.15), channel_id=1, source_target_pairs={{0,128},{16,144},{1,129},{17,145},{2,130},{18,146},{3,131},{19,147... | collective-permute-start | bytes 589832 | tf_op jit(solution)/shard_map/ppermute | solution.py:33
  10.5 32.8 %collective-permute-start.5 = (f32[3,32,2048]{2,1,0:T(8,128)}, f32[3,32,2048]{2,1,0:T(8,128)}, u32[]{:S(2)}, u32[]{:S(2)}) collective-permute-start(f32[3,32,2048]{2,1,0:T(8,128)} %slice.16), channel_id=1, source_target_pairs={{16,32},{17,33},{18,34},{19,35},{20,36},{21,37},{22,38},{23,39},{2... | collective-permute-start | bytes 2359304 | tf_op jit(solution)/shard_map/ppermute | solution.py:33
  20.5 26.9 %collective-permute-start.6 = (f32[3,32,2048]{2,1,0:T(8,128)}, f32[3,32,2048]{2,1,0:T(8,128)}, u32[]{:S(2)}, u32[]{:S(2)}) collective-permute-start(f32[3,32,2048]{2,1,0:T(8,128)} %slice.13), channel_id=1, source_target_pairs={{48,112},{49,113},{50,114},{51,115},{52,116},{53,117},{54,118},{55... | collective-permute-start | bytes 2359304 | tf_op jit(solution)/shard_map/ppermute | solution.py:33
  22.1 25.3 %collective-permute-start.4 = (f32[3,8,2048]{2,1,0:T(8,128)S(1)}, f32[3,8,2048]{2,1,0:T(8,128)}, u32[]{:S(2)}, u32[]{:S(2)}) collective-permute-start(f32[3,8,2048]{2,1,0:T(8,128)S(1)} %add_add_fusion), channel_id=1, source_target_pairs={{0,32},{16,48},{1,33},{17,49},{2,34},{18,50},{3,35},{19,51},{4,36}... | collective-permute-start | bytes 589832 | tf_op jit(solution)/shard_map/ppermute | solution.py:33
  27.4 17.2 %collective-permute-start.7 = (f32[3,1,2048]{2,1,0:T(1,128)S(1)}, f32[3,1,2048]{2,1,0:T(1,128)S(1)}, u32[]{:S(2)}, u32[]{:S(2)}) collective-permute-start(f32[3,1,2048]{2,1,0:T(1,128)S(1)} %get-tuple-element.23), channel_id=1, source_target_pairs={{0,1},{16,17},{1,2},{17,18},{2,3},{18,19},{3,0},{19,16},{4,5},{20,... | collective-permute-start | bytes 73736 | tf_op jit(solution)/shard_map/ppermute | solution.py:33
  28.8 15.8 %collective-permute-start.8 = (f32[3,1,2048]{2,1,0:T(1,128)S(1)}, f32[3,1,2048]{2,1,0:T(1,128)S(1)}, u32[]{:S(2)}, u32[]{:S(2)}) collective-permute-start(f32[3,1,2048]{2,1,0:T(1,128)S(1)} %get-tuple-element.22), channel_id=1, source_target_pairs={{0,3},{16,19},{1,0},{17,16},{2,1},{18,17},{3,2},{19,18},{4,7},{20,... | collective-permute-start | bytes 73736 | tf_op jit(solution)/shard_map/ppermute | solution.py:33
  43.3 33.2 %collective-permute-start.18 = (f32[3,32,2048]{2,1,0:T(8,128)}, f32[3,32,2048]{2,1,0:T(8,128)S(1)}, u32[]{:S(2)}, u32[]{:S(2)}) collective-permute-start(f32[3,32,2048]{2,1,0:T(8,128)} %collective-permute-done.5.crossed_ref), channel_id=1, source_target_pairs={{16,64},{17,65},{18,66},{19,67},{20,68},{21,69},{22,70},{23,71},{2... | collective-permute-start | bytes 2359304 | tf_op jit(solution)/shard_map/ppermute | solution.py:33
  44.7 1.4 %copy-start.2 = (f32[3,64,2048]{2,1,0:T(8,128)S(1)}, f32[3,64,2048]{2,1,0:T(8,128)}, u32[]{:S(2)}) copy-start(f32[3,64,2048]{2,1,0:T(8,128)} %param.3) | copy-start | bytes 4718596
  48.5 28.1 %collective-permute-start.19 = (f32[3,32,2048]{2,1,0:T(8,128)S(1)}, f32[3,32,2048]{2,1,0:T(8,128)S(1)}, u32[]{:S(2)}, u32[]{:S(2)}) collective-permute-start(f32[3,32,2048]{2,1,0:T(8,128)S(1)} %broadcast_select_fusion), channel_id=1, source_target_pairs={{16,32},{17,33},{18,34},{19,35},{20,36},{21,37},{22,38},{23,39},{2... | collective-permute-start | bytes 2359304 | tf_op jit(solution)/shard_map/ppermute | solution.py:33
  57.2 6.4 %collective-permute-start.10 = (f32[3,8,2048]{2,1,0:T(8,128)S(1)}, f32[3,8,2048]{2,1,0:T(8,128)S(1)}, u32[]{:S(2)}, u32[]{:S(2)}) collective-permute-start(f32[3,8,2048]{2,1,0:T(8,128)S(1)} %add_multiply_fusion.p0.refs_0_), channel_id=1, source_target_pairs={{0,128},{16,144},{1,129},{17,145},{2,130},{18,146},{3,131},{19,147... | collective-permute-start | bytes 589832 | tf_op jit(solution)/shard_map/ppermute | solution.py:33
  58.7 7.0 %collective-permute-start.11 = (f32[3,8,2048]{2,1,0:T(8,128)S(1)}, f32[3,8,2048]{2,1,0:T(8,128)S(1)}, u32[]{:S(2)}, u32[]{:S(2)}) collective-permute-start(f32[3,8,2048]{2,1,0:T(8,128)S(1)} %add_multiply_fusion.p0.refs_0_), channel_id=1, source_target_pairs={{0,64},{16,80},{1,65},{17,81},{2,66},{18,82},{3,67},{19,83},{4,68}... | collective-permute-start | bytes 589832 | tf_op jit(solution)/shard_map/ppermute | solution.py:33
  58.7 7.0 %collective-permute-start.9 = (f32[3,8,2048]{2,1,0:T(8,128)S(1)}, f32[3,8,2048]{2,1,0:T(8,128)S(1)}, u32[]{:S(2)}, u32[]{:S(2)}) collective-permute-start(f32[3,8,2048]{2,1,0:T(8,128)S(1)} %add_multiply_fusion.p0.refs_0_), channel_id=1, source_target_pairs={{0,192},{16,208},{1,193},{17,209},{2,194},{18,210},{3,195},{19,211... | collective-permute-start | bytes 589832 | tf_op jit(solution)/shard_map/ppermute | solution.py:33
  63.6 4.1 %collective-permute-start.12 = (f32[3,8,2048]{2,1,0:T(8,128)S(1)}, f32[3,8,2048]{2,1,0:T(8,128)S(1)}, u32[]{:S(2)}, u32[]{:S(2)}) collective-permute-start(f32[3,8,2048]{2,1,0:T(8,128)S(1)} %add_multiply_fusion.p0.refs_0_), channel_id=1, source_target_pairs={{0,16},{16,0},{1,17},{17,1},{2,18},{18,2},{3,19},{19,3},{4,20},{20... | collective-permute-start | bytes 589832 | tf_op jit(solution)/shard_map/ppermute | solution.py:33
  66.3 4.3 %collective-permute-start.16 = (f32[3,1,2048]{2,1,0:T(1,128)S(1)}, f32[3,1,2048]{2,1,0:T(1,128)S(1)}, u32[]{:S(2)}, u32[]{:S(2)}) collective-permute-start(f32[3,1,2048]{2,1,0:T(1,128)S(1)} %edge.1), channel_id=1, source_target_pairs={{0,3},{16,17},{1,0},{17,18},{2,1},{18,19},{3,2},{19,16},{4,7},{20,... | collective-permute-start | bytes 73736 | tf_op jit(solution)/shard_map/ppermute | solution.py:33
  67.7 3.5 %collective-permute-start.17 = (f32[3,1,2048]{2,1,0:T(1,128)S(1)}, f32[3,1,2048]{2,1,0:T(1,128)S(1)}, u32[]{:S(2)}, u32[]{:S(2)}) collective-permute-start(f32[3,1,2048]{2,1,0:T(1,128)S(1)} %edge.1), channel_id=1, source_target_pairs={{0,19},{16,1},{1,16},{17,2},{2,17},{18,3},{3,18},{19,0},{4,23},{20... | collective-permute-start | bytes 73736 | tf_op jit(solution)/shard_map/ppermute | solution.py:33
  67.7 4.6 %collective-permute-start.13 = (f32[3,8,2048]{2,1,0:T(8,128)S(1)}, f32[3,8,2048]{2,1,0:T(8,128)S(1)}, u32[]{:S(2)}, u32[]{:S(2)}) collective-permute-start(f32[3,8,2048]{2,1,0:T(8,128)S(1)} %collective-permute-done.9.p1.refs_1_), channel_id=1, source_target_pairs={{0,16},{16,0},{1,17},{17,1},{2,18},{18,2},{3,19},{19,3},{4,20},{20... | collective-permute-start | bytes 589832 | tf_op jit(solution)/shard_map/ppermute | solution.py:33
  70.6 1.6 %collective-permute-start.14 = (f32[3,8,2048]{2,1,0:T(8,128)S(1)}, f32[3,8,2048]{2,1,0:T(8,128)S(1)}, u32[]{:S(2)}, u32[]{:S(2)}) collective-permute-start(f32[3,8,2048]{2,1,0:T(8,128)S(1)} %collective-permute-done.10.p2.refs_2_), channel_id=1, source_target_pairs={{0,16},{16,0},{1,17},{17,1},{2,18},{18,2},{3,19},{19,3},{4,20},{20... | collective-permute-start | bytes 589832 | tf_op jit(solution)/shard_map/ppermute | solution.py:33
  71.2 2.1 %collective-permute-start.15 = (f32[3,8,2048]{2,1,0:T(8,128)S(1)}, f32[3,8,2048]{2,1,0:T(8,128)S(1)}, u32[]{:S(2)}, u32[]{:S(2)}) collective-permute-start(f32[3,8,2048]{2,1,0:T(8,128)S(1)} %collective-permute-done.11.p3.refs_3_), channel_id=1, source_target_pairs={{0,16},{16,0},{1,17},{17,1},{2,18},{18,2},{3,19},{19,3},{4,20},{20... | collective-permute-start | bytes 589832 | tf_op jit(solution)/shard_map/ppermute | solution.py:33
